TPU v7x, 32 devices: a whole 2x2x4 slice. The times are simulated.
32 devices in a mesh: grp: 2 (over x), mk: 8 (over z, y), tile: 2 (over core).
Axes of the slice: x: 2, y: 2, z: 4, core: 2. Of those that a mesh axis runs over, the one named last changes fastest.
Arguments:
- dosage: bfloat16 [3072, 16384], P(('grp', 'tile'), 'mk'), parts along dimension 0, may hold values from 0 to 2
- allele_freq: float32 [32768], P(('grp', 'mk')), parts along dimension 0, may hold values from 0.05 to 0.5
- present: int32 [256, 3072], P('mk', ('grp', 'tile')), parts along dimension 1, may hold values 0 or 1
- panel_rows: int32 [32], P('grp'), parts along dimension 0, may hold values from 1 to 192, 1536 in all
Outputs:
- panels: float32 [6144, 1536], P(('grp', 'mk', 'tile')), parts along dimension 0
There are 2 independent parts, one for each index of `grp`. A program takes and returns all parts, laid end to end along the dimension named above; each array names one. Nothing has to cross between parts.
Inputs may be any that keep to these rules, and one draw needn't show every extreme that they name: `panel_rows`: the counts sum to 1536.
All inputs are finite; a program needn't handle non-finite values. No bound on the sum of `present` on one device may be relied on, other than what follows from the above.
Results may differ from a plain program's by a relative error of at most 0.0011.
Values may be sent and summed in bfloat16 or wider, within the bound.
A program may use at most 64 MiB of HBM per device.

v0:
```python
import jax
import jax.numpy as jnp
from jax import lax
from jax.sharding import PartitionSpec as P


def local(dosage, allele_freq, present, panel_rows):
    tile_count = lax.axis_size("tile")
    local_markers = dosage.shape[1]
    marker_total = local_markers * lax.axis_size("mk")
    flags = jnp.repeat(present.T, local_markers // present.shape[0], axis=1).astype(jnp.float32)
    twice_freq = 2.0 * allele_freq
    scaled = (dosage.astype(jnp.float32) - twice_freq) / jnp.sqrt(twice_freq * (1.0 - allele_freq))
    standard = (flags * scaled).astype(jnp.bfloat16)
    all_rows = lax.all_gather(standard, "tile", axis=0, tiled=True)
    samples = all_rows.shape[0]
    owner_count = lax.axis_size("mk") * tile_count
    panel_max = 2 * samples // owner_count
    starts = jnp.cumsum(panel_rows) - panel_rows
    row_ids = jnp.arange(panel_max * tile_count * lax.axis_size("mk"), dtype=jnp.int32)
    owner_ids = row_ids // panel_max
    within = row_ids - owner_ids * panel_max
    sample_ids = jnp.take(starts, owner_ids) + within
    live = within < jnp.take(panel_rows, owner_ids)
    picked = jnp.take(all_rows, jnp.clip(sample_ids, 0, samples - 1), axis=0)
    picked = jnp.where(live[:, None], picked, jnp.zeros((), jnp.bfloat16))
    product = jnp.einsum("rm,sm->rs", picked, standard, preferred_element_type=jnp.float32)
    pair_rows = lax.psum_scatter(
        product * (1.0 / marker_total), "mk", scatter_dimension=0, tiled=True
    )
    return lax.all_to_all(pair_rows, "tile", split_axis=0, concat_axis=1, tiled=True)


def solution(mesh):
    in_specs = (P(("grp", "tile"), "mk"), P(("grp", "mk")), P("mk", ("grp", "tile")), P("grp"))
    out_specs = P(("grp", "mk", "tile"), None)
    return jax.shard_map(local, mesh=mesh, in_specs=in_specs, out_specs=out_specs, check_vma=False)
```

profile of v0, /device:TPU:0, one launch (start us, length us, event | category | flops | bytes accessed | tf_op | source)
XLA Modules:
  0.0 279.3 jit_solution(269421417285457136)
XLA Ops:
  6.5 0.0 all-gather.2.cloned.1.call-start
  6.5 0.7 broadcast_multiply_fusion
  7.2 0.9 convert_bitcast_fusion
  8.1 3.1 %broadcast_in_dim.38 = f32[768,32,64]{0,2,1:T(8,128)} broadcast(f32[768,32]{0,1:T(8,128)S(1)} %convert_bitcast_fusion), dimensions={0,1} | broadcast | bytes 6389760 | tf_op jit(solution)/shard_map/broadcast_in_dim | solution.py:11
  11.3 0.0 copy-start.1
  11.3 6.7 %copy.9 = f32[768,2048]{1,0:T(8,128)} copy(f32[768,2048]{0,1:T(8,128)} %bitcast.41) | data formatting | bytes 12582912 | tf_op jit(solution)/shard_map/convert_element_type | solution.py:11
  18.0 0.0 copy-done.1
  18.0 0.0 copy-start.2
  18.0 5.6 %multiply_convert_fusion = bf16[768,2048]{1,0:T(8,128)(2,1)} fusion(f32[768,2048]{1,0:T(8,128)} %copy.9, bf16[768,2048]{1,0:T(8,128)(2,1)S(1)} %copy-done.1, f32[2048]{0:T(1024)S(1)} %get-tuple-element.7, f32[2048]{0:T(1024)S(1)} %get-tuple-element.6), kind=kLoop, calls=%fused_computation.8 | loop fusion | flops 7864320 | bytes 12599296 | tf_op jit(solution)/shard_map/convert_element_type | solution.py:14
  23.6 0.0 all-gather.2.cloned.1.call-update
  23.7 0.0 reduce-scatter.2.cloned.1.call-start
  23.7 0.0 copy-done.2
  23.7 0.1 copy.8
  23.9 0.1 reduce
  24.0 0.7 fusion.17
  24.7 9.9 %compare_and_fusion.1 = pred[3072]{0:T(1024)(128)(4,1)S(1)} fusion(s32[]{:T(128)} %bitcast.32, s32[]{:T(128)} %bitcast.31, s32[]{:T(128)} %bitcast.30, s32[]{:T(128)} %bitcast.29, s32[]{:T(128)} %bitcast.28, s32[]{:T(128)} %bitcast.27, s32[]{:T(128)} %bitcast.26, s32[]{:T(128)} %bitcast.25, s32[]{:T(128)} %bitcast.24, s32[]{:T(128)} %bitcast.23, ...), kind=kLoop, calls=%fused_computation.25 | loop fusion | flops 168960 | bytes 3136 | tf_op jit(solution)/shard_map/jit(_take)/and | solution.py:25
  34.6 0.7 fusion.16
  35.3 10.2 %select_compare_fusion = pred[3072]{0:T(1024)(128)(4,1)S(1)} fusion(s32[]{:T(128)} %bitcast.15, s32[]{:T(128)} %bitcast.14, s32[]{:T(128)} %bitcast.13, s32[]{:T(128)} %bitcast.12, s32[]{:T(128)} %bitcast.11, s32[]{:T(128)} %bitcast.10, s32[]{:T(128)} %bitcast.9, s32[]{:T(128)} %bitcast.8, s32[]{:T(128)} %bitcast.7, s32[]{:T(128)} %bitcast.6, s32[]{:T(128)} %bitcast.5, ...), kind=kLoop, calls=%fused_computation.22 | loop fusion | flops 147456 | bytes 3136 | tf_op jit(solution)/shard_map/lt | solution.py:24
  45.5 9.9 %broadcast_clamp_fusion = s32[3072]{0:T(1024)S(1)} fusion(s32[]{:T(128)} %bitcast.32, s32[]{:T(128)} %bitcast.31, s32[]{:T(128)} %bitcast.30, s32[]{:T(128)} %bitcast.29, s32[]{:T(128)} %bitcast.28, s32[]{:T(128)} %bitcast.27, s32[]{:T(128)} %bitcast.26, s32[]{:T(128)} %bitcast.25, s32[]{:T(128)} %bitcast.24, s32[]{:T(128)} %bitcast.23, s32[]{:T(128)} %bitcast.22, ...), kind=kLoop, calls=%fused_computation.27 | loop fusion | flops 162816 | bytes 12352 | tf_op jit(solution)/shard_map/jit(_take)/gather | solution.py:25
  55.4 0.0 copy-start
  55.4 0.0 all-gather.2.cloned.1.call-done
  55.5 27.6 %gather_fusion = bf16[3072,2048]{1,0:T(8,128)(2,1)} fusion(bf16[1536,2048]{1,0:T(8,128)(2,1)} %all-gather.2.cloned.1.call-done, s32[3072]{0:T(1024)S(1)} %broadcast_clamp_fusion), kind=kCustom, calls=%fused_computation | custom fusion | bytes 25178112 | tf_op jit(solution)/shard_map/jit(_take)/gather | solution.py:25
  83.0 0.0 copy-done
  83.0 16.2 %fusion.7 = f32[3072,768]{1,0:T(8,128)} fusion(bf16[768,2048]{1,0:T(8,128)(2,1)S(1)} %copy-done, bf16[3072,2048]{1,0:T(8,128)(2,1)} %gather_fusion, pred[3072]{0:T(1024)(128)(4,1)S(1)} %compare_and_fusion.1, pred[3072]{0:T(1024)(128)(4,1)S(1)} %select_compare_fusion), kind=kOutput, calls=%fused_computation.9 | convolution fusion | flops 9678618624 | bytes 25171968 | tf_op jit(solution)/shard_map/rm,sm->rs/dot_general | solution.py:27
  99.2 0.0 reduce-scatter.2.cloned.1.call-update
  99.2 166.3 %reduce-scatter.2.cloned.1.call-done = f32[384,768]{1,0:T(8,128)} async-done(((f32[3072,768]{1,0:T(8,128)}), f32[384,768]{1,0:T(8,128)}) %reduce-scatter.2.cloned.1.call-update) | async-done | bytes 1179664 | tf_op jit(solution)/shard_map/reduce_scatter | solution.py:28
  265.5 5.8 %all_to_all.19 = f32[2,192,768]{2,1,0:T(8,128)S(1)} all-to-all(f32[2,192,768]{2,1,0:T(8,128)} %bitcast.43), channel_id=1, replica_groups=mesh['grp'=2,'mk'=8,'tile'=2] {'tile'}, dimensions={0} | all-to-all | bytes 2359296 | tf_op jit(solution)/shard_map/all_to_all | solution.py:31
  271.3 1.2 copy.11
  (2 shorter events, 0.0 us)
Async XLA Ops:
  6.5 48.9 %all-gather.2.cloned.1.call-start = ((), (), s32[]{:S(2)}) async-start(), calls=%async_computation.2 | async-start | bytes 9437184 | tf_op jit(solution)/shard_map/all_gather | solution.py:15
  11.3 6.7 %copy-start.1 = (bf16[768,2048]{1,0:T(8,128)(2,1)S(1)}, bf16[768,2048]{1,0:T(8,128)(2,1)}, u32[]{:S(2)}) copy-start(bf16[768,2048]{1,0:T(8,128)(2,1)} %param.6) | copy-start | bytes 9437188
  18.0 5.7 %copy-start.2 = (s32[16]{0:T(128)S(1)}, s32[16]{0:T(128)}, u32[]{:S(2)}) copy-start(s32[16]{0:T(128)} %param.9) | copy-start | bytes 196
  23.7 241.8 %reduce-scatter.2.cloned.1.call-start = ((), (), s32[]{:S(2)}) async-start(), calls=%async_computation.3 | async-start | bytes 10616832 | tf_op jit(solution)/shard_map/reduce_scatter | solution.py:28
  55.4 27.6 %copy-start = (bf16[768,2048]{1,0:T(8,128)(2,1)S(1)}, bf16[768,2048]{1,0:T(8,128)(2,1)}, u32[]{:S(2)}) copy-start(bf16[768,2048]{1,0:T(8,128)(2,1)} %multiply_convert_fusion) | copy-start | bytes 9437188
Sparse Core Ops, SparseCore 0:
  23.8 19.4 all-gather.1
  99.3 166.0 reduce-scatter.1
where the time goes:
time: 280 us; the launch traced here: 279 us
  waiting for transfers between devices  166 us (59%)
  local copies, waits for them, and re-layouts  40.1 us (14%)
  other arithmetic  37.4 us (13%)
  matrix products  16.2 us (6%)
  between operations  13.5 us (5%)
  blocking collectives  5.8 us (2%)
    reduce_scatter x1, waiting for transfers between devices, local(): lax.psum_scatter(product * (1.0 / marker_total), 'mk', scatter_dimension=...  166 us
    gather x1, local copies, waits for them, and re-layouts, local(): picked = jnp.take(all_rows, jnp.clip(sample_ids, 0, samples - 1), axis=0)  27.6 us
    dot_general x1, matrix products, local(): jnp.einsum('rm,sm->rs', picked, standard, preferred_element_type=jnp.floa...  16.2 us
    lt x1, other arithmetic, local(): live = within < jnp.take(panel_rows, owner_ids)  10.2 us
    and x1, other arithmetic, local(): picked = jnp.take(all_rows, jnp.clip(sample_ids, 0, samples - 1), axis=0)  9.9 us
    gather x1, other arithmetic, local(): picked = jnp.take(all_rows, jnp.clip(sample_ids, 0, samples - 1), axis=0)  9.88 us
    convert_element_type x1, local copies, waits for them, and re-layouts, local(): jnp.repeat(present.T, local_markers // present.shape[0], axis=1)  6.71 us
    all_to_all x1, blocking collectives, local(): lax.all_to_all(pair_rows, 'tile', split_axis=0, concat_axis=1, tiled=True)  5.8 us
  transfers between devices with their start and end apart: 2, of which 1 were waited for; matrix products, arithmetic and copies ran while one was open for 11% of the time, Pallas kernels for 0%

commit v1 on v0

--- a/solution.py
+++ b/solution.py
@@ -28,7 +28,12 @@
     pair_rows = lax.psum_scatter(
         product * (1.0 / marker_total), "mk", scatter_dimension=0, tiled=True
     )
-    return lax.all_to_all(pair_rows, "tile", split_axis=0, concat_axis=1, tiled=True)
+    return jnp.concatenate(
+        lax.all_to_all(
+            jnp.stack(jnp.split(pair_rows, lax.axis_size("tile"), axis=0)), "tile", 0, 0
+        ),
+        axis=1,
+    )
 
 
 def solution(mesh):

time: 280 us -> 280 us (level)
  no operation moved by 1% of the time
where the time goes in v1:
time: 280 us
  waiting for transfers between devices  166 us (59%)
  local copies, waits for them, and re-layouts  41.5 us (15%)
  other arithmetic  37.6 us (13%)
  matrix products  16.1 us (6%)
  between operations  13.5 us (5%)
  blocking collectives  4.68 us (2%)
    reduce_scatter x1, waiting for transfers between devices, local(): lax.psum_scatter(product * (1.0 / marker_total), 'mk', scatter_dimension=...  166 us
    gather x1, local copies, waits for them, and re-layouts, local(): picked = jnp.take(all_rows, jnp.clip(sample_ids, 0, samples - 1), axis=0)  27.6 us
    dot_general x1, matrix products, local(): jnp.einsum('rm,sm->rs', picked, standard, preferred_element_type=jnp.floa...  16.1 us
    lt x1, other arithmetic, local(): live = within < jnp.take(panel_rows, owner_ids)  10.1 us
    and x1, other arithmetic, local(): picked = jnp.take(all_rows, jnp.clip(sample_ids, 0, samples - 1), axis=0)  9.97 us
    gather x1, other arithmetic, local(): picked = jnp.take(all_rows, jnp.clip(sample_ids, 0, samples - 1), axis=0)  9.96 us
    convert_element_type x1, local copies, waits for them, and re-layouts, local(): jnp.repeat(present.T, local_markers // present.shape[0], axis=1)  6.78 us
    convert_element_type x1, other arithmetic, local(): standard = (flags * scaled).astype(jnp.bfloat16)  5.63 us
  transfers between devices with their start and end apart: 2, of which 1 were waited for; matrix products, arithmetic and copies ran while one was open for 11% of the time, Pallas kernels for 0%

profile of v1, /device:TPU:0, one launch (start us, length us, event | category | flops | bytes accessed | tf_op | source)
XLA Modules:
  0.0 279.8 jit_solution(1414188013923625936)
XLA Ops:
  6.5 0.0 all-gather.2.cloned.1.call-start
  6.5 0.7 broadcast_multiply_fusion
  7.2 0.9 convert_bitcast_fusion
  8.1 3.1 %broadcast_in_dim.38 = f32[768,32,64]{0,2,1:T(8,128)} broadcast(f32[768,32]{0,1:T(8,128)S(1)} %convert_bitcast_fusion), dimensions={0,1} | broadcast | bytes 6389760 | tf_op jit(solution)/shard_map/broadcast_in_dim | solution.py:11
  11.3 0.0 copy-start.1
  11.3 6.8 %copy.8 = f32[768,2048]{1,0:T(8,128)} copy(f32[768,2048]{0,1:T(8,128)} %bitcast.44) | data formatting | bytes 12582912 | tf_op jit(solution)/shard_map/convert_element_type | solution.py:11
  18.1 0.0 copy-done.1
  18.1 0.0 copy-start.2
  18.1 5.6 %multiply_convert_fusion = bf16[768,2048]{1,0:T(8,128)(2,1)} fusion(f32[768,2048]{1,0:T(8,128)} %copy.8, bf16[768,2048]{1,0:T(8,128)(2,1)S(1)} %copy-done.1, f32[2048]{0:T(1024)S(1)} %get-tuple-element.9, f32[2048]{0:T(1024)S(1)} %get-tuple-element.8), kind=kLoop, calls=%fused_computation.8 | loop fusion | flops 7864320 | bytes 12599296 | tf_op jit(solution)/shard_map/convert_element_type | solution.py:14
  23.7 0.0 all-gather.2.cloned.1.call-update
  23.7 0.0 reduce-scatter.2.cloned.1.call-start
  23.8 0.0 copy-done.2
  23.8 0.1 copy.7
  23.9 0.1 reduce
  24.0 0.7 fusion.17
  24.7 10.0 %compare_and_fusion.1 = pred[3072]{0:T(1024)(128)(4,1)S(1)} fusion(s32[]{:T(128)} %bitcast.32, s32[]{:T(128)} %bitcast.31, s32[]{:T(128)} %bitcast.30, s32[]{:T(128)} %bitcast.29, s32[]{:T(128)} %bitcast.28, s32[]{:T(128)} %bitcast.27, s32[]{:T(128)} %bitcast.26, s32[]{:T(128)} %bitcast.25, s32[]{:T(128)} %bitcast.24, s32[]{:T(128)} %bitcast.23, ...), kind=kLoop, calls=%fused_computation.28 | loop fusion | flops 168960 | bytes 3136 | tf_op jit(solution)/shard_map/jit(_take)/and | solution.py:25
  34.7 0.7 fusion.16
  35.4 10.1 %select_compare_fusion = pred[3072]{0:T(1024)(128)(4,1)S(1)} fusion(s32[]{:T(128)} %bitcast.15, s32[]{:T(128)} %bitcast.14, s32[]{:T(128)} %bitcast.13, s32[]{:T(128)} %bitcast.12, s32[]{:T(128)} %bitcast.11, s32[]{:T(128)} %bitcast.10, s32[]{:T(128)} %bitcast.9, s32[]{:T(128)} %bitcast.8, s32[]{:T(128)} %bitcast.7, s32[]{:T(128)} %bitcast.6, s32[]{:T(128)} %bitcast.5, ...), kind=kLoop, calls=%fused_computation.25 | loop fusion | flops 147456 | bytes 3136 | tf_op jit(solution)/shard_map/lt | solution.py:24
  45.6 10.0 %broadcast_clamp_fusion = s32[3072]{0:T(1024)S(1)} fusion(s32[]{:T(128)} %bitcast.32, s32[]{:T(128)} %bitcast.31, s32[]{:T(128)} %bitcast.30, s32[]{:T(128)} %bitcast.29, s32[]{:T(128)} %bitcast.28, s32[]{:T(128)} %bitcast.27, s32[]{:T(128)} %bitcast.26, s32[]{:T(128)} %bitcast.25, s32[]{:T(128)} %bitcast.24, s32[]{:T(128)} %bitcast.23, s32[]{:T(128)} %bitcast.22, ...), kind=kLoop, calls=%fused_computation.30 | loop fusion | flops 162816 | bytes 12352 | tf_op jit(solution)/shard_map/jit(_take)/gather | solution.py:25
  55.6 0.0 copy-start
  55.6 0.0 all-gather.2.cloned.1.call-done
  55.6 27.6 %gather_fusion = bf16[3072,2048]{1,0:T(8,128)(2,1)} fusion(bf16[1536,2048]{1,0:T(8,128)(2,1)} %all-gather.2.cloned.1.call-done, s32[3072]{0:T(1024)S(1)} %broadcast_clamp_fusion), kind=kCustom, calls=%fused_computation | custom fusion | bytes 25178112 | tf_op jit(solution)/shard_map/jit(_take)/gather | solution.py:25
  83.2 0.0 copy-done
  83.2 16.1 %fusion.7 = f32[3072,768]{1,0:T(8,128)} fusion(bf16[768,2048]{1,0:T(8,128)(2,1)S(1)} %copy-done, bf16[3072,2048]{1,0:T(8,128)(2,1)} %gather_fusion, pred[3072]{0:T(1024)(128)(4,1)S(1)} %compare_and_fusion.1, pred[3072]{0:T(1024)(128)(4,1)S(1)} %select_compare_fusion), kind=kOutput, calls=%fused_computation.9 | convolution fusion | flops 9678618624 | bytes 25171968 | tf_op jit(solution)/shard_map/rm,sm->rs/dot_general | solution.py:27
  99.3 0.0 reduce-scatter.2.cloned.1.call-update
  99.3 166.3 %reduce-scatter.2.cloned.1.call-done = f32[384,768]{1,0:T(8,128)} async-done(((f32[3072,768]{1,0:T(8,128)}), f32[384,768]{1,0:T(8,128)}) %reduce-scatter.2.cloned.1.call-update) | async-done | bytes 1179664 | tf_op jit(solution)/shard_map/reduce_scatter | solution.py:28
  265.7 1.3 slice_bitcast_fusion.1
  267.0 0.1 pad_maximum_fusion
  267.1 4.7 %all_to_all.5 = f32[2,192,768]{2,1,0:T(8,128)S(1)} all-to-all(f32[2,192,768]{2,1,0:T(8,128)S(1)} %pad_maximum_fusion), channel_id=1, replica_groups=mesh['grp'=2,'mk'=8,'tile'=2] {'tile'}, dimensions={0} | all-to-all | bytes 2359296 | tf_op jit(solution)/shard_map/all_to_all | solution.py:32
  271.8 1.2 copy.10
  (2 shorter events, 0.0 us)
Async XLA Ops:
  6.5 49.1 %all-gather.2.cloned.1.call-start = ((), (), s32[]{:S(2)}) async-start(), calls=%async_computation.2 | async-start | bytes 9437184 | tf_op jit(solution)/shard_map/all_gather | solution.py:15
  11.3 6.8 %copy-start.1 = (bf16[768,2048]{1,0:T(8,128)(2,1)S(1)}, bf16[768,2048]{1,0:T(8,128)(2,1)}, u32[]{:S(2)}) copy-start(bf16[768,2048]{1,0:T(8,128)(2,1)} %param.6) | copy-start | bytes 9437188
  18.1 5.7 %copy-start.2 = (s32[16]{0:T(128)S(1)}, s32[16]{0:T(128)}, u32[]{:S(2)}) copy-start(s32[16]{0:T(128)} %param.9) | copy-start | bytes 196
  23.7 241.9 %reduce-scatter.2.cloned.1.call-start = ((), (), s32[]{:S(2)}) async-start(), calls=%async_computation.3 | async-start | bytes 10616832 | tf_op jit(solution)/shard_map/reduce_scatter | solution.py:28
  55.6 27.6 %copy-start = (bf16[768,2048]{1,0:T(8,128)(2,1)S(1)}, bf16[768,2048]{1,0:T(8,128)(2,1)}, u32[]{:S(2)}) copy-start(bf16[768,2048]{1,0:T(8,128)(2,1)} %multiply_convert_fusion) | copy-start | bytes 9437188
Sparse Core Ops, SparseCore 0:
  23.9 19.4 all-gather.1
  99.5 166.1 reduce-scatter.1
